TPU v7x, 256 devices: a whole 4x4x8 slice. The times are simulated.
256 devices in a mesh: prompt: 8 (over z_hi, core), resp: 16 (over y, x), grp: 2 (over z_lo).
Axes of the slice: x: 4, y: 4, z: 8 (z_hi: 4, z_lo: 2; z = z_hi * 2 + z_lo), core: 2. Of those that a mesh axis runs over, the one named last changes fastest.
Arguments:
- queries: bfloat16 [32, 1024, 4096], P(('grp', 'resp'), 'prompt'), parts along dimension 0, may hold values from -5 to 5
- response_key_rows: bfloat16 [32, 1024, 512], P(('grp', 'resp'), 'prompt'), parts along dimension 0, may hold values from -6 to 6
- response_value_rows: bfloat16 [32, 1024, 512], P(('grp', 'resp'), 'prompt'), parts along dimension 0, may hold values from -24 to 24
- prompt_keys: bfloat16 [2048, 512], P(('grp', 'prompt', 'resp')), parts along dimension 0, may hold values from -18 to 18
- prompt_value_rows: bfloat16 [2048, 512], P(('grp', 'prompt', 'resp')), parts along dimension 0, may hold values from -24 to 24
- out_grad: bfloat16 [32, 1024, 4096], P(('grp', 'resp'), 'prompt'), parts along dimension 0, may hold values from -6 to 6
- lengths: int32 [32], P('grp'), parts along dimension 0, may hold values from 128 to 1024
Outputs:
- attended: bfloat16 [32, 1024, 4096], P(('grp', 'resp'), 'prompt'), parts along dimension 0
- query_grad: bfloat16 [32, 1024, 4096], P(('grp', 'resp'), 'prompt'), parts along dimension 0
- resp_key_grad: bfloat16 [32, 1024, 512], P(('grp', 'resp'), 'prompt'), parts along dimension 0
- resp_value_grad: bfloat16 [32, 1024, 512], P(('grp', 'resp'), 'prompt'), parts along dimension 0
- prompt_key_grad: float32 [2048, 512], P(('grp', 'prompt', 'resp')), parts along dimension 0
- prompt_value_grad: float32 [2048, 512], P(('grp', 'prompt', 'resp')), parts along dimension 0
There are 2 independent parts, one for each index of `grp`. A program takes and returns all parts, laid end to end along the dimension named above; each array names one. Nothing has to cross between parts.
All inputs are finite; a program needn't handle non-finite values.
Results may differ from a plain program's by a relative error of at most 0.02.
The roundings to bfloat16 on the way count: a program that leaves them out, or rounds other values in their place, can miss the bound.
Values may be sent and summed in bfloat16 or wider, within the bound.
A program may use at most 128 MiB of HBM per device.

v0:
```python
import functools

import jax
import jax.numpy as jnp
from jax import lax
from jax.experimental import pallas as pl
from jax.experimental.pallas import tpu as pltpu
from jax.sharding import PartitionSpec as P

F32 = jnp.float32
BF16 = jnp.bfloat16
MESH = pl.DeviceIdType.MESH

HEADS = 4
GROUP = 8
D = 128
RT = 128
SIDE = 4
CHUNK = 4
SCALE = D**-0.5
SCALE_LOG2E = SCALE * 1.4426950408889634

NT = (((1,), (1,)), ((), ()))
NN = (((1,), (0,)), ((), ()))
TN = (((0,), (0,)), ((), ()))


def dot(a, b, dims):
    return lax.dot_general(a, b, dims, preferred_element_type=F32)


def kernel(
    q_ref, g_ref, kr_ref, vr_ref, pk_ref, pv_ref, len_ref,
    o_ref, dq_ref, drk_ref, drv_ref, dpk_ref, dpv_ref,
    q_buf, g_buf, q_sem, g_sem, KT, VT, DS, bias, xs, xr, G, RB, AP, AR, T, c0r, c1r, c2r, c3r, d0r, d1r, fin, fr,
    a0_s, a0_r, a1_s, a1_r, a2_s, a2_r, a3_s, a3_r, a4_s, a4_r, b_s, b_r, bs_s, bs_r,
    c0_s, c0_r, c1_s, c1_r, c2_s, c2_r, c3_s, c3_r, c4_s, c4_r, d0_s, d0_r, d1_s, d1_r,
):
    p = lax.axis_index("prompt")
    r = lax.axis_index("resp")
    c = p % 2
    o = 1 - c
    zh = p // 2
    y = r // SIDE
    x = r % SIDE
    sib = {"prompt": zh * 2 + o}

    def z_peer(k):
        return {"prompt": ((zh + k) % SIDE) * 2 + c}

    def y_peer(k):
        return {"resp": ((y + k) % SIDE) * SIDE + x}

    def x_peer(k):
        return {"resp": y * SIDE + (x + k) % SIDE}

    def remote(src, dst, ss, rs, dev):
        return pltpu.make_async_remote_copy(
            src_ref=src, dst_ref=dst, send_sem=ss, recv_sem=rs, device_id=dev, device_id_type=MESH
        )

    peers = [sib] + [f(k) for f in (z_peer, y_peer, x_peer) for k in (1, 2, 3)]
    barrier = pltpu.get_barrier_semaphore()
    for dev in peers:
        pl.semaphore_signal(barrier, inc=1, device_id=dev, device_id_type=MESH)
    mine_k = pk_ref[...].astype(F32)
    mine_v = pv_ref[...].astype(F32)
    is0 = c == 0
    xs[...] = jnp.where(is0, mine_v, mine_k)
    mine = jnp.where(is0, mine_k, mine_v)
    for h in range(HEADS):
        cols = slice(h * D, (h + 1) * D)
        RB[h, 0, p] = kr_ref[:, cols]
        RB[h, 1, p] = vr_ref[:, cols]
    pl.semaphore_wait(barrier, len(peers))

    def a0():
        return remote(xs, xr, a0_s, a0_r, sib)

    def a1(k):
        block = G.at[c, :, zh, y, x]
        return remote(block, block, a1_s.at[k - 1], a1_r.at[k - 1], z_peer(k))

    def a2(h, k):
        block = G.at[c, h, :, y, x]
        dev = {"resp": jnp.where(is0, y_peer(k)["resp"], x_peer(k)["resp"])}
        return remote(block, block, a2_s.at[h, k - 1], a2_r.at[h, k - 1], dev)

    def a3(h, k, core):
        block, dev = (G.at[0, h, :, :, x], x_peer(k)) if core == 0 else (G.at[1, h, :, y], y_peer(k))
        return remote(block, block, a3_s.at[h, k - 1], a3_r.at[h, k - 1], dev)

    def a4(h):
        return remote(G.at[c, h], G.at[c, h], a4_s.at[h], a4_r.at[h], sib)

    def b(h, k):
        return remote(RB.at[h, :, p], RB.at[h, :, p], b_s.at[h, k - 1], b_r.at[h, k - 1], z_peer(k))

    def b_sib(h, k):
        block = RB.at[h, :, ((zh - k + SIDE) % SIDE) * 2 + c]
        return remote(block, block, bs_s.at[h, k], bs_r.at[h, k], sib)

    def c0(h):
        return remote(AP.at[h, o], c0r.at[h], c0_s.at[h], c0_r.at[h], sib)

    def c1(h, k, core):
        if core == 0:
            block, dev = AP.at[h, 0, :, :, (x + k) % SIDE], x_peer(k)
        else:
            block, dev = AP.at[h, 1, :, (y + k) % SIDE], y_peer(k)
        return remote(block, c1r.at[h, k - 1], c1_s.at[h, k - 1], c1_r.at[h, k - 1], dev)

    def c2(h, k):
        to_y = jnp.where(is0, (y + k) % SIDE, y)
        to_x = jnp.where(is0, x, (x + k) % SIDE)
        return remote(
            AP.at[h, c, :, to_y, to_x], c2r.at[h, k - 1], c2_s.at[h, k - 1], c2_r.at[h, k - 1],
            {"resp": to_y * SIDE + to_x},
        )

    def c3(h, k):
        return remote(
            AP.at[h, c, (zh + k) % SIDE, y, x], c3r.at[h, k - 1], c3_s.at[h, k - 1], c3_r.at[h, k - 1], z_peer(k)
        )

    def c4():
        return remote(fin.at[o], fr, c4_s, c4_r, sib)

    def d0(h):
        return remote(T.at[h, :, o], d0r.at[h], d0_s.at[h], d0_r.at[h], sib)

    def d1(h, k):
        to = (zh - k + SIDE) % SIDE
        return remote(T.at[h, to, c], d1r.at[h, k - 1], d1_s.at[h, k - 1], d1_r.at[h, k - 1], {"prompt": to * 2 + c})

    def on_cores(f):
        pl.when(is0)(lambda: f(0))
        pl.when(c == 1)(lambda: f(1))

    def start_b(h):
        b_sib(h, 0).start()
        for k in (1, 2, 3):
            pl.when(zh + k < SIDE)(lambda k=k: b(h, k).start())

    def a2_to_a3(h):
        for k in (1, 2, 3):
            a2(h, k).wait_recv()

        def send(core):
            for k in (1, 2, 3):
                a3(h, k, core).start()

        on_cores(send)

    def relay(h):
        for k in (1, 2, 3):
            a3(h, k, 0).wait_recv()
        a4(h).start()
        for k in (1, 2, 3):

            def pass_on(k=k):
                b(h, k).wait_recv()
                b_sib(h, k).start()

            pl.when(zh - k >= 0)(pass_on)

    def have_resp(h):
        b_sib(h, 0).wait_recv()
        for k in (1, 2, 3):
            pl.when(zh - k >= 0)(lambda k=k: b_sib(h, k).wait_recv())

    def terms_out(h):
        T[h, :, :, 0] = (AR[0] * SCALE).astype(BF16).reshape(SIDE, 2, RT, D)
        T[h, :, :, 1] = AR[1].astype(BF16).reshape(SIDE, 2, RT, D)
        d0(h).start()

    def step1(h):
        step1_prompt(h)
        step1_resp(h)

    def step1_prompt(h):
        c0(h).wait_recv()
        AP[h, c] += c0r[h]

        def send(core):
            for k in (1, 2, 3):
                c1(h, k, core).start()

        on_cores(send)

    def step1_resp(h):
        d0(h).wait_recv()
        for k in (1, 2, 3):

            def pair(k=k):
                T[h, zh - k, c] = (T[h, zh - k, c].astype(F32) + d0r[h, zh - k].astype(F32)).astype(BF16)
                d1(h, k).start()

            pl.when(zh - k >= 0)(pair)

    def step2(h):
        for k in (1, 2, 3):
            c1(h, k, 0).wait_recv()
        total = c1r[h, 0] + c1r[h, 1] + c1r[h, 2]

        def add(core):
            if core == 0:
                AP[h, 0, :, :, x] += total
            else:
                AP[h, 1, :, y] += total

        on_cores(add)
        for k in (1, 2, 3):
            c2(h, k).start()

    def step3(h):
        for k in (1, 2, 3):
            c2(h, k).wait_recv()
        AP[h, c, :, y, x] += c2r[h, 0] + c2r[h, 1] + c2r[h, 2]
        for k in (1, 2, 3):
            c3(h, k).start()

    def step4(h):
        for k in (1, 2, 3):
            pl.when(zh + k < SIDE)(lambda k=k: d1(h, k).wait_recv())
        terms = T[h, zh, c].astype(F32) + d0r[h, zh].astype(F32)
        terms = terms + d1r[h, 0].astype(F32) + d1r[h, 1].astype(F32) + d1r[h, 2].astype(F32)
        cols = pl.ds(pl.multiple_of(h * D, D), D)
        drk_ref[:, cols] = terms[0].astype(BF16)
        drv_ref[:, cols] = terms[1].astype(BF16)
        for k in (1, 2, 3):
            c3(h, k).wait_recv()
        total = AP[h, c, zh, y, x] + c3r[h, 0] + c3r[h, 1] + c3r[h, 2]
        total = total * jnp.where(is0, SCALE, 1.0).astype(F32)
        fin[:, :, cols] = total.reshape(2, 8, D)

    a0().start()
    q_in = pltpu.make_async_copy(q_ref, q_buf, q_sem)
    g_in = pltpu.make_async_copy(g_ref, g_buf, g_sem)
    q_in.start()
    g_in.start()
    for k in (1, 2, 3):

        def clear_b(k=k):
            RB[:, :, pl.ds((zh + k) * 2, 2)] = jnp.zeros((HEADS, 2, 2, RT, D), BF16)

        pl.when(zh + k < SIDE)(clear_b)

        def clear_d(k=k):
            d1r[:, k - 1] = jnp.zeros((HEADS, 2, RT, D), BF16)

        pl.when(zh + k >= SIDE)(clear_d)

    a0().wait_recv()
    theirs = xr[...]
    rows = jnp.concatenate([jnp.where(is0, mine, theirs), jnp.where(is0, theirs, mine)], 0).astype(BF16)
    for h in range(HEADS):
        G[c, h, zh, y, x] = rows[:, h * D : (h + 1) * D]
    for k in (1, 2, 3):
        a1(k).start()
    start_b(0)
    place = lax.broadcasted_iota(jnp.int32, (SIDE * 2 * RT, RT), 1) + p * RT
    key_place = lax.broadcasted_iota(jnp.int32, (SIDE * 2 * RT, RT), 0)
    bias[...] = jnp.where(key_place <= place, 0.0, -1e30).astype(F32)
    length = len_ref[r]
    live = (lax.broadcasted_iota(jnp.int32, (RT, 1), 0) + p * RT < length).astype(F32).astype(BF16)
    live = jnp.concatenate([live] * CHUNK, 0)
    live_cols = (lax.broadcasted_iota(jnp.int32, (1, RT), 1) + p * RT < length).astype(F32)
    live_cols = jnp.concatenate([live_cols] * CHUNK, 1)
    for k in (1, 2, 3):
        a1(k).wait_recv()
    for k in (1, 2, 3):
        a2(0, k).start()
    a2_to_a3(0)
    for h in range(1, HEADS):
        for k in (1, 2, 3):
            a2(h, k).start()
    q_in.wait()
    g_in.wait()
    relay(0)
    for h in range(1, HEADS):
        a2_to_a3(h)
    start_b(1)

    def dq_part(h, i):
        for_rows = dot(KT[h], DS[h % 2, i], NN) * SCALE
        for j in range(CHUNK):
            col = pl.ds(pl.multiple_of(h * GROUP * D + (i * CHUNK + j) * D, D), D)
            dq_ref[:, col] = for_rows[:, j * RT : (j + 1) * RT].T.astype(BF16)

    def head(h, _):
        keys = SIDE * 2 * RT
        a4(h).wait_recv()
        kp, vp = (G[t, h].reshape(-1, D) for t in (0, 1))
        KT[h, :, :keys] = kp.T
        VT[:, :keys] = vp.T

        def tick(n):
            if n == 0:
                pl.when(h > 0)(lambda: step1(h - 1))
                pl.when(h < HEADS - 2)(lambda: start_b(h + 2))
            if n == 1:
                pl.when(h > 1)(lambda: step3(h - 2))
                pl.when(h < HEADS - 1)(lambda: relay(h + 1))
            if n == 2:
                pl.when(h > 2)(lambda: step4(h - 3))
            if n == 3:
                pl.when(h > 0)(lambda: step2(h - 1))

        for i in range(GROUP // CHUNK):
            cols = [pl.ds(pl.multiple_of(h * GROUP * D + (i * CHUNK + j) * D, D), D) for j in range(CHUNK)]
            qs = jnp.concatenate([q_buf[:, col] for col in cols], 0)
            gs = jnp.concatenate([g_buf[:, col] for col in cols], 0) * live
            sp = dot(kp, qs, NT)
            dpp = dot(vp, gs, NT)
            if i == 0:
                have_resp(h)
            kr, vr = (RB[h, t].reshape(-1, D) for t in (0, 1))
            if i == 0:
                KT[h, :, keys:] = kr.T
                VT[:, keys:] = vr.T
            sr = dot(kr, qs, NT) + jnp.concatenate([bias[...]] * CHUNK, 1)
            dpr = dot(vr, gs, NT)
            top = jnp.maximum(jnp.max(sp, 0, keepdims=True), jnp.max(sr, 0, keepdims=True))
            top = top * SCALE_LOG2E
            wp = jnp.exp2(sp * SCALE_LOG2E - top)
            wr = jnp.exp2(sr * SCALE_LOG2E - top)
            inv = 1.0 / (jnp.sum(wp, 0, keepdims=True) + jnp.sum(wr, 0, keepdims=True))
            pp = wp * inv
            pr = wr * inv
            php = pp.astype(BF16)
            phr = pr.astype(BF16)
            out = dot(VT[:, :keys], php, NN) + dot(VT[:, keys:], phr, NN)
            out = (out * live_cols).astype(BF16).astype(F32)
            for j, col in enumerate(cols):
                o_ref[:, col] = out[:, j * RT : (j + 1) * RT].T.astype(BF16)
            row_dot = jnp.sum(gs.astype(F32).T * out, 0, keepdims=True)
            tick(2 * i)
            dsp = (pp * (dpp - row_dot)).astype(BF16)
            dsr = (pr * (dpr - row_dot)).astype(BF16)
            DS[h % 2, i, :keys] = dsp
            DS[h % 2, i, keys:] = dsr
            for t, new in ((0, dot(dsp, qs, NN)), (1, dot(php, gs, NN))):
                new = new.reshape(SIDE, SIDE, SIDE, 16, D)
                if i == 0:
                    AP[h, t] = new
                else:
                    AP[h, t] += new
            if i == GROUP // CHUNK - 1:
                c0(h).start()
            for t, new in ((0, dot(dsr, qs, NN)), (1, dot(phr, gs, NN))):
                if i == 0:
                    AR[t] = new
                else:
                    AR[t] += new
            if i == GROUP // CHUNK - 1:
                terms_out(h)
            tick(2 * i + 1)

        def dq_now():
            for i in range(GROUP // CHUNK):
                dq_part(h, i)

        pl.when(h < 2)(dq_now)
        return 0

    lax.fori_loop(0, HEADS, head, 0)
    dq_part(2, 0)
    step1_prompt(3)
    dq_part(2, 1)
    step1_resp(3)
    step3(2)
    dq_part(3, 0)
    dq_part(3, 1)
    step4(1)
    step4(2)
    step2(3)
    step3(3)
    step4(3)
    c4().start()
    c4().wait_recv()
    own = fin[c]
    other = fr[...]
    dpk_ref[...] = jnp.where(is0, own, other)
    dpv_ref[...] = jnp.where(is0, other, own)

    a0().wait_send()
    c4().wait_send()
    for k in (1, 2, 3):
        a1(k).wait_send()

    def sent(h, _):
        a4(h).wait_send()
        c0(h).wait_send()
        d0(h).wait_send()
        b_sib(h, 0).wait_send()
        for k in (1, 2, 3):
            a2(h, k).wait_send()
            a3(h, k, 0).wait_send()
            c1(h, k, 0).wait_send()
            c2(h, k).wait_send()
            c3(h, k).wait_send()

            def conditional(k=k):
                b_sib(h, k).wait_send()
                d1(h, k).wait_send()

            pl.when(zh - k >= 0)(conditional)
            pl.when(zh + k < SIDE)(lambda k=k: b(h, k).wait_send())
        return 0

    lax.fori_loop(0, HEADS, sent, 0)


def hand_over(*refs):
    n = (len(refs) - 1) // 2
    copies = [pltpu.make_async_copy(refs[i], refs[n + i], refs[-1].at[i]) for i in range(n)]
    for copy in copies:
        copy.start()
    for copy in copies:
        copy.wait()


def body(queries, response_key_rows, response_value_rows, prompt_keys, prompt_value_rows, out_grad, lengths):
    dma = pltpu.SemaphoreType.DMA
    vmem = pl.BlockSpec(memory_space=pltpu.VMEM)
    hbm = pl.BlockSpec(memory_space=pl.ANY)
    scratch = [
        pltpu.VMEM((RT, HEADS * GROUP * D), BF16),
        pltpu.VMEM((RT, HEADS * GROUP * D), BF16),
        dma,
        dma,
        pltpu.VMEM((HEADS, D, 16 * RT), BF16),
        pltpu.VMEM((D, 16 * RT), BF16),
        pltpu.VMEM((2, GROUP // CHUNK, 16 * RT, CHUNK * RT), BF16),
        pltpu.VMEM((8 * RT, RT), F32),
        pltpu.VMEM((8, HEADS * D), F32),
        pltpu.VMEM((8, HEADS * D), F32),
        pltpu.VMEM((2, HEADS, SIDE, SIDE, SIDE, 16, D), BF16),
        pltpu.VMEM((HEADS, 2, 8, RT, D), BF16),
        pltpu.VMEM((HEADS, 2, SIDE, SIDE, SIDE, 16, D), F32),
        pltpu.VMEM((2, 8 * RT, D), F32),
        pltpu.VMEM((HEADS, SIDE, 2, 2, RT, D), BF16),
        pltpu.VMEM((HEADS, SIDE, SIDE, SIDE, 16, D), F32),
        pltpu.VMEM((HEADS, 3, SIDE, SIDE, 16, D), F32),
        pltpu.VMEM((HEADS, 3, SIDE, 16, D), F32),
        pltpu.VMEM((HEADS, 3, 16, D), F32),
        pltpu.VMEM((HEADS, SIDE, 2, RT, D), BF16),
        pltpu.VMEM((HEADS, 3, 2, RT, D), BF16),
        pltpu.VMEM((2, 8, HEADS * D), F32),
        pltpu.VMEM((8, HEADS * D), F32),
    ]
    per_peer = dma((HEADS, 3))
    per_head = dma((HEADS,))
    sems = [dma, dma, dma((3,)), dma((3,)), per_peer, per_peer, per_peer, per_peer, per_head, per_head]
    sems += [per_peer, per_peer, dma((HEADS, 4)), dma((HEADS, 4))]
    sems += [per_head, per_head] + [per_peer] * 6 + [dma, dma, per_head, per_head, per_peer, per_peer]
    wide = jax.ShapeDtypeStruct(queries.shape[1:], BF16)
    rows = jax.ShapeDtypeStruct(response_key_rows.shape[1:], BF16)
    shared = jax.ShapeDtypeStruct(prompt_keys.shape, F32)
    shapes = [wide, wide, rows, rows, shared, shared]
    results = pl.pallas_call(
        kernel,
        out_shape=shapes,
        in_specs=[hbm] * 2 + [vmem] * 4 + [pl.BlockSpec(memory_space=pltpu.SMEM)],
        out_specs=[vmem] * 6,
        scratch_shapes=scratch + sems,
        compiler_params=pltpu.CompilerParams(
            collective_id=0, has_side_effects=True, vmem_limit_bytes=60 * 2**20
        ),
        cost_estimate=pl.CostEstimate(flops=13 * 10**9, bytes_accessed=5 * 2**20, transcendentals=2**23),
    )(queries[0], out_grad[0], response_key_rows[0], response_value_rows[0], prompt_keys, prompt_value_rows, lengths)
    out, dq, drk, drv, dpk, dpv = pl.pallas_call(
        hand_over,
        out_shape=shapes,
        in_specs=[vmem] * 6,
        out_specs=[hbm] * 6,
        scratch_shapes=[dma((6,))],
    )(*results)
    return out[None], dq[None], drk[None], drv[None], dpk, dpv


def solution(mesh):
    rows = P(("grp", "resp"), "prompt", None)
    shared = P(("grp", "prompt", "resp"), None)
    return jax.shard_map(
        body,
        mesh=mesh,
        in_specs=(rows, rows, rows, shared, shared, rows, P("grp")),
        out_specs=(rows, rows, rows, rows, shared, shared),
        check_vma=False,
    )
```

profile of v0, /device:TPU:1, one launch (start us, length us, event | category | flops | bytes accessed | tf_op | source)
XLA Modules:
  0.0 95.0 jit_solution(11579528506519975970)
XLA Ops:
  0.6 91.3 %shard_map.118 = (bf16[128,4096]{1,0:T(8,128)(2,1)}, bf16[128,4096]{1,0:T(8,128)(2,1)}, bf16[128,512]{1,0:T(8,128)(2,1)}, bf16[128,512]{1,0:T(8,128)(2,1)}, f32[8,512]{1,0:T(8,128)}, /*index=5*/f32[8,512]{1,0:T(8,128)}) custom-call(bf16[128,4096]{1,0:T(8,128)(2,1)} %bitcast.8, bf16[128,4096]{1,0:T(8,128)(2,1)} %bitcast.9, bf16[128,512]{1,0:T(8,128)(2,1)} %bitcast.12, ...), custom_call_target="tpu_custom_call" | custom-call | flops 12999999488 | bytes 5242880 | tf_op jit(solution)/shard_map/pallas_call | solution.py:462
  91.9 3.0 %shard_map.119 = (bf16[128,4096]{1,0:T(8,128)(2,1)}, bf16[128,4096]{1,0:T(8,128)(2,1)}, bf16[128,512]{1,0:T(8,128)(2,1)}, bf16[128,512]{1,0:T(8,128)(2,1)}, f32[8,512]{1,0:T(8,128)}, /*index=5*/f32[8,512]{1,0:T(8,128)}) custom-call(bf16[128,4096]{1,0:T(8,128)(2,1)} %get-tuple-element.18.refs_0_, bf16[128,4096]{1,0:T(8,128)(2,1)} %get-tuple-element.19.refs_1_, ...), custom_call_target="tpu_custom_call" | custom-call | tf_op jit(solution)/shard_map/pallas_call | solution.py:473
where the time goes:
time: 95.1 us; the launch traced here: 95 us
  Pallas kernels  94.3 us (99%)
    pallas_call x1, Pallas kernels, body(): pl.pallas_call(kernel, out_shape=shapes, in_specs=[hbm] * 2 + [vmem] * 4...  91.3 us
    pallas_call x1, Pallas kernels, body(): pl.pallas_call(hand_over, out_shape=shapes, in_specs=[vmem] * 6, out_spec...  3.03 us

commit v1 on v0

v1 whole, which is shorter than its diff:
```python
import functools

import jax
import jax.numpy as jnp
from jax import lax
from jax.experimental import pallas as pl
from jax.experimental.pallas import tpu as pltpu
from jax.sharding import PartitionSpec as P

F32 = jnp.float32
BF16 = jnp.bfloat16
MESH = pl.DeviceIdType.MESH

HEADS = 4
GROUP = 8
D = 128
RT = 128
SIDE = 4
PLANE = 16
SLOTS = 4
TILE = 256
KEYS = 1024
SCALE = D**-0.5
SCALE_LOG2E = SCALE * 1.4426950408889634

NT = (((1,), (1,)), ((), ()))
NN = (((1,), (0,)), ((), ()))
TN = (((0,), (0,)), ((), ()))


def dot(a, b, dims):
    return lax.dot_general(a, b, dims, preferred_element_type=F32)


def kernel(
    q_ref, g_ref, kr_ref, vr_ref, pk_ref, pv_ref, len_ref,
    o_ref, dq_ref, drk_ref, drv_ref, dpk_ref, dpv_ref,
    q_buf, g_buf, q_sem, g_sem, KV, KT, VT, DS, bias, G, RB, AP, T, c0r, c1r, c2r, d0r, d1r,
    a1_s, a1_r, a2_s, a2_r, a3_s, a3_r, b_s, b_r, bs_s, bs_r,
    c0_s, c0_r, c1_s, c1_r, c2_s, c2_r, d0_s, d0_r, d1_s, d1_r,
):
    p = lax.axis_index("prompt")
    r = lax.axis_index("resp")
    c = p % 2
    o = 1 - c
    zh = p // 2
    sib = {"prompt": zh * 2 + o}

    def z_peer(k):
        return {"prompt": ((zh + k) % SIDE) * 2 + c}

    def plane_peer(j):
        return {"resp": (r + j) % PLANE}

    def remote(src, dst, ss, rs, dev):
        return pltpu.make_async_remote_copy(
            src_ref=src, dst_ref=dst, send_sem=ss, recv_sem=rs, device_id=dev, device_id_type=MESH
        )

    peers = [sib] + [z_peer(k) for k in (1, 2, 3)] + [plane_peer(j) for j in range(1, PLANE)]
    barrier = pltpu.get_barrier_semaphore()
    for dev in peers:
        pl.semaphore_signal(barrier, inc=1, device_id=dev, device_id_type=MESH)
    mine = jnp.concatenate([pk_ref[...].astype(F32), pv_ref[...].astype(F32)], 0).astype(BF16)
    for h in range(HEADS):
        cols = slice(h * D, (h + 1) * D)
        RB[h, 0, p] = kr_ref[:, cols]
        RB[h, 1, p] = vr_ref[:, cols]
        G[c, h, r, zh] = mine[:, cols]
    pl.semaphore_wait(barrier, len(peers))

    def a1(part, k):
        block = G.at[c, 0:1, r, zh] if part == 0 else G.at[c, 1:HEADS, r, zh]
        return remote(block, block, a1_s.at[part, k - 1], a1_r.at[part, k - 1], z_peer(k))

    def a2_start(h):
        def send(j, _):
            remote(G.at[c, h, r], G.at[c, h, r], a2_s.at[h], a2_r.at[h], plane_peer(j)).start()
            return 0

        lax.fori_loop(1, PLANE, send, 0)

    def a2_all(h):
        rows = G.at[c, h, 0 : PLANE - 1]
        return remote(rows, rows, a2_s.at[h], a2_r.at[h], sib)

    def a3(h):
        return remote(G.at[c, h], G.at[c, h], a3_s.at[h], a3_r.at[h], sib)

    def b(h, t, k):
        return remote(RB.at[h, t, p], RB.at[h, t, p], b_s.at[h, t, k - 1], b_r.at[h, t, k - 1], z_peer(k))

    def b_sib(h, t, k):
        block = RB.at[h, t, ((zh - k + SIDE) % SIDE) * 2 + c]
        return remote(block, block, bs_s.at[h, t, k], bs_r.at[h, t, k], sib)

    def c0(h):
        return remote(AP.at[h, o], c0r.at[h], c0_s.at[h], c0_r.at[h], sib)

    def c1_start(h):
        def send(j, _):
            to = (r + j) % PLANE
            remote(AP.at[h, c, :, to], c1r.at[h, j - 1], c1_s.at[h], c1_r.at[h], {"resp": to}).start()
            return 0

        lax.fori_loop(1, PLANE, send, 0)

    def c1_all(h):
        return remote(c1r.at[h], c1r.at[h], c1_s.at[h], c1_r.at[h], sib)

    def c2(h, k):
        to = (zh + k) % SIDE
        return remote(AP.at[h, c, :, r, to], c2r.at[h, k - 1], c2_s.at[h, k - 1], c2_r.at[h, k - 1], z_peer(k))

    def d0(h):
        return remote(T.at[h, :, o], d0r.at[h], d0_s.at[h], d0_r.at[h], sib)

    def d1(h, k):
        to = (zh - k + SIDE) % SIDE
        return remote(T.at[h, to, c], d1r.at[h, k - 1], d1_s.at[h, k - 1], d1_r.at[h, k - 1], {"prompt": to * 2 + c})

    def start_b(h):
        for t in (0, 1):
            b_sib(h, t, 0).start()
            for k in (1, 2, 3):
                pl.when(zh + k < SIDE)(lambda t=t, k=k: b(h, t, k).start())

    def relay_prompt(h):
        a2_all(h).wait_recv()
        a3(h).start()

    def relay_resp(h, t):
        for k in (1, 2, 3):

            def pass_on(k=k):
                b(h, t, k).wait_recv()
                b_sib(h, t, k).start()

            pl.when(zh - k >= 0)(pass_on)

    def have_resp(h, t):
        b_sib(h, t, 0).wait_recv()
        for k in (1, 2, 3):
            pl.when(zh - k >= 0)(lambda k=k: b_sib(h, t, k).wait_recv())

    def step1(h):
        step1_prompt(h)
        step1_resp(h)

    def step1_prompt(h):
        c0(h).wait_recv()
        AP[h, c] += c0r[h]
        c1_start(h)

    def step1_resp(h):
        d0(h).wait_recv()
        for k in (1, 2, 3):

            def pair(k=k):
                T[h, zh - k, c] = (T[h, zh - k, c].astype(F32) + d0r[h, zh - k].astype(F32)).astype(BF16)
                d1(h, k).start()

            pl.when(zh - k >= 0)(pair)

    def step2(h):
        c1_all(h).wait_recv()
        total = AP[h, c, :, r]
        for j in range(PLANE - 1):
            total = total + c1r[h, j]
        AP[h, c, :, r] = total
        for k in (1, 2, 3):
            c2(h, k).start()

    def step3(h):
        for k in (1, 2, 3):
            pl.when(zh + k < SIDE)(lambda k=k: d1(h, k).wait_recv())
        terms = T[h, zh, c].astype(F32) + d0r[h, zh].astype(F32)
        terms = terms + d1r[h, 0].astype(F32) + d1r[h, 1].astype(F32) + d1r[h, 2].astype(F32)
        cols = pl.ds(pl.multiple_of(h * D, D), D)
        drk_ref[:, cols] = terms[0].astype(BF16)
        drv_ref[:, cols] = terms[1].astype(BF16)
        for k in (1, 2, 3):
            c2(h, k).wait_recv()
        total = AP[h, c, :, r, zh] + c2r[h, 0] + c2r[h, 1] + c2r[h, 2]
        dpk_ref[:, cols] = total[0] * SCALE
        dpv_ref[:, cols] = total[1]

    for part in (0, 1):
        for k in (1, 2, 3):
            a1(part, k).start()
    start_b(0)
    q_in = pltpu.make_async_copy(q_ref, q_buf, q_sem)
    g_in = pltpu.make_async_copy(g_ref, g_buf, g_sem)
    q_in.start()
    g_in.start()
    for k in (1, 2, 3):
        a1(0, k).wait_recv()
    a2_start(0)
    for k in (1, 2, 3):

        def clear_b(k=k):
            RB[:, :, pl.ds((zh + k) * 2, 2)] = jnp.zeros((HEADS, 2, 2, RT, D), BF16)

        pl.when(zh + k < SIDE)(clear_b)

        def clear_d(k=k):
            d1r[:, k - 1] = jnp.zeros((HEADS, 2, RT, D), BF16)

        pl.when(zh + k >= SIDE)(clear_d)

    for k in (1, 2, 3):
        a1(1, k).wait_recv()
    for h in range(1, HEADS):
        a2_start(h)
    place = lax.broadcasted_iota(jnp.int32, (SIDE * 2 * RT, RT), 1) + p * RT
    key_place = lax.broadcasted_iota(jnp.int32, (SIDE * 2 * RT, RT), 0)
    bias[...] = jnp.where(key_place <= place, 0.0, -1e30).astype(F32)
    length = len_ref[r]
    live = (lax.broadcasted_iota(jnp.int32, (RT, 1), 0) + p * RT < length).astype(F32).astype(BF16)
    live = jnp.concatenate([live] * GROUP, 0)
    live_cols = (lax.broadcasted_iota(jnp.int32, (1, RT), 1) + p * RT < length).astype(F32)
    live_cols = jnp.concatenate([live_cols] * GROUP, 1)
    q_in.wait()
    g_in.wait()
    relay_prompt(0)
    relay_resp(0, 0)
    start_b(1)

    def dq_part(h):
        for_rows = dot(KT[h], DS[h % SLOTS], NN) * SCALE
        for j in range(GROUP):
            col = pl.ds(pl.multiple_of((h * GROUP + j) * D, D), D)
            dq_ref[:, col] = for_rows[:, j * RT : (j + 1) * RT].T.astype(BF16)

    def head(h, _):
        a3(h).wait_recv()
        for lane in (0, 1):
            rows = slice(lane * KEYS // 2, (lane + 1) * KEYS // 2)
            blocks = G[lane, h].astype(F32).reshape(PLANE * SIDE, 2, 8, D)
            KV[0, rows] = blocks[:, 0].reshape(-1, D).astype(BF16)
            KV[1, rows] = blocks[:, 1].reshape(-1, D).astype(BF16)
        kp, vp = KV[0], KV[1]
        KT[h, :, :KEYS] = kp.T
        VT[:, :KEYS] = vp.T
        cols = [pl.ds(pl.multiple_of((h * GROUP + j) * D, D), D) for j in range(GROUP)]
        qs = jnp.concatenate([q_buf[:, col] for col in cols], 0)
        gs = jnp.concatenate([g_buf[:, col] for col in cols], 0) * live

        tiles = [slice(first, first + TILE) for first in range(0, KEYS, TILE)]
        scores = [dot(kp[tile], qs, NT) for tile in tiles]
        top = functools.reduce(jnp.maximum, [jnp.max(score, 0, keepdims=True) for score in scores])
        have_resp(h, 0)
        kr = RB[h, 0].reshape(-1, D)
        KT[h, :, KEYS:] = kr.T
        for tile in tiles:
            score = dot(kr[tile], qs, NT) + jnp.concatenate([bias[tile]] * GROUP, 1)
            top = jnp.maximum(top, jnp.max(score, 0, keepdims=True))
            scores.append(score)
        pl.when(h > 0)(lambda: step1(h - 1))
        pl.when(h == 0)(lambda: relay_resp(h, 1))
        pl.when(h < HEADS - 2)(lambda: start_b(h + 2))
        top = top * SCALE_LOG2E
        weights = [jnp.exp2(score * SCALE_LOG2E - top) for score in scores]
        inv = 1.0 / functools.reduce(jnp.add, [jnp.sum(weight, 0, keepdims=True) for weight in weights])

        def after_weights():
            relay_prompt(h + 1)
            relay_resp(h + 1, 0)
            relay_resp(h + 1, 1)

        pl.when(h < HEADS - 1)(after_weights)
        have_resp(h, 1)
        vr = RB[h, 1].reshape(-1, D)
        VT[:, KEYS:] = vr.T
        probs = [weight * inv for weight in weights]
        halves = [prob.astype(BF16) for prob in probs]
        out = functools.reduce(
            jnp.add, [dot(VT[:, i * TILE : (i + 1) * TILE], half, NN) for i, half in enumerate(halves)]
        )
        out = (out * live_cols).astype(BF16).astype(F32)
        for j, col in enumerate(cols):
            o_ref[:, col] = out[:, j * RT : (j + 1) * RT].T.astype(BF16)
        row_dot = jnp.sum(gs.astype(F32).T * out, 0, keepdims=True)
        pl.when(h > 1)(lambda: step3(h - 2))

        def tile_grads(i, values):
            ds = (probs[i] * (dot(values, gs, NT) - row_dot)).astype(BF16)
            DS[h % SLOTS, i * TILE : (i + 1) * TILE] = ds
            return dot(ds, qs, NN), dot(halves[i], gs, NN)

        for i, tile in enumerate(tiles):
            grads = tile_grads(i, vp[tile])
            for t in (0, 1):
                AP[h, i // 2, t, i % 2 * 8 : i % 2 * 8 + 8] = grads[t].reshape(8, SIDE, 8, D)
        c0(h).start()
        pl.when(h > 0)(lambda: step2(h - 1))
        for i, tile in enumerate(tiles):
            for_keys, for_values = tile_grads(len(tiles) + i, vr[tile])
            T[h, i, :, 0] = (for_keys * SCALE).astype(BF16).reshape(2, RT, D)
            T[h, i, :, 1] = for_values.astype(BF16).reshape(2, RT, D)
        d0(h).start()
        return 0

    lax.fori_loop(0, HEADS, head, 0)
    dq_part(0)
    step1_prompt(3)
    step1_resp(3)
    dq_part(1)
    step3(2)
    dq_part(2)
    dq_part(3)
    step2(3)
    step3(3)

    for k in (1, 2, 3):
        a1(0, k).wait_send()
        a1(1, k).wait_send()

    def sent(h, _):
        a2_all(h).wait_send()
        a3(h).wait_send()
        c1_all(h).wait_send()
        c0(h).wait_send()
        d0(h).wait_send()
        b_sib(h, 0, 0).wait_send()
        b_sib(h, 1, 0).wait_send()
        for k in (1, 2, 3):
            c2(h, k).wait_send()

            def conditional(k=k):
                b_sib(h, 0, k).wait_send()
                b_sib(h, 1, k).wait_send()
                d1(h, k).wait_send()

            pl.when(zh - k >= 0)(conditional)

            def sent_on(k=k):
                b(h, 0, k).wait_send()
                b(h, 1, k).wait_send()

            pl.when(zh + k < SIDE)(sent_on)
        return 0

    lax.fori_loop(0, HEADS, sent, 0)


def hand_over(*refs):
    n = (len(refs) - 1) // 2
    copies = [pltpu.make_async_copy(refs[i], refs[n + i], refs[-1].at[i]) for i in range(n)]
    for copy in copies:
        copy.start()
    for copy in copies:
        copy.wait()


def body(queries, response_key_rows, response_value_rows, prompt_keys, prompt_value_rows, out_grad, lengths):
    dma = pltpu.SemaphoreType.DMA
    vmem = pl.BlockSpec(memory_space=pltpu.VMEM)
    hbm = pl.BlockSpec(memory_space=pl.ANY)
    scratch = [
        pltpu.VMEM((RT, HEADS * GROUP * D), BF16),
        pltpu.VMEM((RT, HEADS * GROUP * D), BF16),
        dma,
        dma,
        pltpu.VMEM((2, KEYS, D), BF16),
        pltpu.VMEM((HEADS, D, 2 * KEYS), BF16),
        pltpu.VMEM((D, 2 * KEYS), BF16),
        pltpu.VMEM((SLOTS, 2 * KEYS, GROUP * RT), BF16),
        pltpu.VMEM((8 * RT, RT), F32),
        pltpu.VMEM((2, HEADS, PLANE, SIDE, 16, D), BF16),
        pltpu.VMEM((HEADS, 2, 8, RT, D), BF16),
        pltpu.VMEM((HEADS, 2, 2, PLANE, SIDE, 8, D), F32),
        pltpu.VMEM((HEADS, SIDE, 2, 2, RT, D), BF16),
        pltpu.VMEM((HEADS, 2, PLANE, SIDE, 8, D), F32),
        pltpu.VMEM((HEADS, PLANE - 1, 2, SIDE, 8, D), F32),
        pltpu.VMEM((HEADS, 3, 2, 8, D), F32),
        pltpu.VMEM((HEADS, SIDE, 2, RT, D), BF16),
        pltpu.VMEM((HEADS, 3, 2, RT, D), BF16),
    ]
    per_peer = dma((HEADS, 3))
    per_head = dma((HEADS,))
    sems = [dma((2, 3))] * 2 + [per_head] * 4 + [dma((HEADS, 2, 3))] * 2 + [dma((HEADS, 2, 4))] * 2
    sems += [per_head] * 4 + [per_peer] * 2 + [per_head] * 2 + [per_peer] * 2
    wide = jax.ShapeDtypeStruct(queries.shape[1:], BF16)
    rows = jax.ShapeDtypeStruct(response_key_rows.shape[1:], BF16)
    shared = jax.ShapeDtypeStruct(prompt_keys.shape, F32)
    shapes = [wide, wide, rows, rows, shared, shared]
    results = pl.pallas_call(
        kernel,
        out_shape=shapes,
        in_specs=[hbm] * 2 + [vmem] * 4 + [pl.BlockSpec(memory_space=pltpu.SMEM)],
        out_specs=[vmem] * 6,
        scratch_shapes=scratch + sems,
        compiler_params=pltpu.CompilerParams(
            collective_id=0, has_side_effects=True, vmem_limit_bytes=60 * 2**20
        ),
        cost_estimate=pl.CostEstimate(flops=13 * 10**9, bytes_accessed=5 * 2**20, transcendentals=2**23),
    )(queries[0], out_grad[0], response_key_rows[0], response_value_rows[0], prompt_keys, prompt_value_rows, lengths)
    out, dq, drk, drv, dpk, dpv = pl.pallas_call(
        hand_over,
        out_shape=shapes,
        in_specs=[vmem] * 6,
        out_specs=[hbm] * 6,
        scratch_shapes=[dma((6,))],
    )(*results)
    return out[None], dq[None], drk[None], drv[None], dpk, dpv


def solution(mesh):
    rows = P(("grp", "resp"), "prompt", None)
    shared = P(("grp", "prompt", "resp"), None)
    return jax.shard_map(
        body,
        mesh=mesh,
        in_specs=(rows, rows, rows, shared, shared, rows, P("grp")),
        out_specs=(rows, rows, rows, rows, shared, shared),
        check_vma=False,
    )
```

time: 95.1 us -> 88.4 us (0.930)
  the two profiles are of different devices: /device:TPU:1 before, /device:TPU:8 now
where the time goes in v1:
time: 88.4 us; the launch traced here: 88.3 us
  Pallas kernels  87.5 us (99%)
    pallas_call x1, Pallas kernels, body(): pl.pallas_call(kernel, out_shape=shapes, in_specs=[hbm] * 2 + [vmem] * 4...  84.5 us
    pallas_call x1, Pallas kernels, body(): pl.pallas_call(hand_over, out_shape=shapes, in_specs=[vmem] * 6, out_spec...  3.03 us

profile of v1, /device:TPU:8, one launch (start us, length us, event | category | flops | bytes accessed | tf_op | source)
XLA Modules:
  0.0 88.3 jit_solution(15062580288415906569)
XLA Ops:
  0.6 84.5 %shard_map.118 = (bf16[128,4096]{1,0:T(8,128)(2,1)}, bf16[128,4096]{1,0:T(8,128)(2,1)}, bf16[128,512]{1,0:T(8,128)(2,1)}, bf16[128,512]{1,0:T(8,128)(2,1)}, f32[8,512]{1,0:T(8,128)}, /*index=5*/f32[8,512]{1,0:T(8,128)}) custom-call(bf16[128,4096]{1,0:T(8,128)(2,1)} %bitcast.8, bf16[128,4096]{1,0:T(8,128)(2,1)} %bitcast.9, bf16[128,512]{1,0:T(8,128)(2,1)} %bitcast.12, ...), custom_call_target="tpu_custom_call" | custom-call | flops 12999999488 | bytes 5242880 | tf_op jit(solution)/shard_map/pallas_call | solution.py:388
  85.1 3.0 %shard_map.119 = (bf16[128,4096]{1,0:T(8,128)(2,1)}, bf16[128,4096]{1,0:T(8,128)(2,1)}, bf16[128,512]{1,0:T(8,128)(2,1)}, bf16[128,512]{1,0:T(8,128)(2,1)}, f32[8,512]{1,0:T(8,128)}, /*index=5*/f32[8,512]{1,0:T(8,128)}) custom-call(bf16[128,4096]{1,0:T(8,128)(2,1)} %get-tuple-element.18.refs_0_, bf16[128,4096]{1,0:T(8,128)(2,1)} %get-tuple-element.19.refs_1_, ...), custom_call_target="tpu_custom_call" | custom-call | tf_op jit(solution)/shard_map/pallas_call | solution.py:399

commit v2 on v1

--- a/solution.py
+++ b/solution.py
@@ -94,30 +94,32 @@
         block = RB.at[h, t, ((zh - k + SIDE) % SIDE) * 2 + c]
         return remote(block, block, bs_s.at[h, t, k], bs_r.at[h, t, k], sib)
 
-    def c0(h):
-        return remote(AP.at[h, o], c0r.at[h], c0_s.at[h], c0_r.at[h], sib)
-
-    def c1_start(h):
+    def c0(h, t):
+        return remote(AP.at[h, o, t], c0r.at[h, t], c0_s.at[h, t], c0_r.at[h, t], sib)
+
+    def c1_start(h, t):
         def send(j, _):
             to = (r + j) % PLANE
-            remote(AP.at[h, c, :, to], c1r.at[h, j - 1], c1_s.at[h], c1_r.at[h], {"resp": to}).start()
+            remote(AP.at[h, c, t, to], c1r.at[h, t, j - 1], c1_s.at[h, t], c1_r.at[h, t], {"resp": to}).start()
             return 0
 
         lax.fori_loop(1, PLANE, send, 0)
 
-    def c1_all(h):
-        return remote(c1r.at[h], c1r.at[h], c1_s.at[h], c1_r.at[h], sib)
+    def c1_all(h, t):
+        return remote(c1r.at[h, t], c1r.at[h, t], c1_s.at[h, t], c1_r.at[h, t], sib)
 
     def c2(h, k):
         to = (zh + k) % SIDE
         return remote(AP.at[h, c, :, r, to], c2r.at[h, k - 1], c2_s.at[h, k - 1], c2_r.at[h, k - 1], z_peer(k))
 
-    def d0(h):
-        return remote(T.at[h, :, o], d0r.at[h], d0_s.at[h], d0_r.at[h], sib)
-
-    def d1(h, k):
+    def d0(h, t):
+        return remote(T.at[h, :, o, t], d0r.at[h, t], d0_s.at[h, t], d0_r.at[h, t], sib)
+
+    def d1(h, t, k):
         to = (zh - k + SIDE) % SIDE
-        return remote(T.at[h, to, c], d1r.at[h, k - 1], d1_s.at[h, k - 1], d1_r.at[h, k - 1], {"prompt": to * 2 + c})
+        return remote(
+            T.at[h, to, c, t], d1r.at[h, k - 1, t], d1_s.at[h, t, k - 1], d1_r.at[h, t, k - 1], {"prompt": to * 2 + c}
+        )
 
     def start_b(h):
         for t in (0, 1):
@@ -143,38 +145,38 @@
         for k in (1, 2, 3):
             pl.when(zh - k >= 0)(lambda k=k: b_sib(h, t, k).wait_recv())
 
-    def step1(h):
-        step1_prompt(h)
-        step1_resp(h)
-
-    def step1_prompt(h):
-        c0(h).wait_recv()
-        AP[h, c] += c0r[h]
-        c1_start(h)
-
-    def step1_resp(h):
-        d0(h).wait_recv()
+    def step1(h, t):
+        c0(h, t).wait_recv()
+        AP[h, c, t] += c0r[h, t]
+        c1_start(h, t)
+        d0(h, t).wait_recv()
         for k in (1, 2, 3):
 
             def pair(k=k):
-                T[h, zh - k, c] = (T[h, zh - k, c].astype(F32) + d0r[h, zh - k].astype(F32)).astype(BF16)
-                d1(h, k).start()
+                T[h, zh - k, c, t] = (T[h, zh - k, c, t].astype(F32) + d0r[h, t, zh - k].astype(F32)).astype(BF16)
+                d1(h, t, k).start()
 
             pl.when(zh - k >= 0)(pair)
 
     def step2(h):
-        c1_all(h).wait_recv()
+        c1_all(h, 0).wait_recv()
+        c1_all(h, 1).wait_recv()
         total = AP[h, c, :, r]
         for j in range(PLANE - 1):
-            total = total + c1r[h, j]
+            total = total + c1r[h, :, j]
         AP[h, c, :, r] = total
         for k in (1, 2, 3):
             c2(h, k).start()
 
     def step3(h):
         for k in (1, 2, 3):
-            pl.when(zh + k < SIDE)(lambda k=k: d1(h, k).wait_recv())
-        terms = T[h, zh, c].astype(F32) + d0r[h, zh].astype(F32)
+
+            def arrived(k=k):
+                d1(h, 0, k).wait_recv()
+                d1(h, 1, k).wait_recv()
+
+            pl.when(zh + k < SIDE)(arrived)
+        terms = T[h, zh, c].astype(F32) + d0r[h, :, zh].astype(F32)
         terms = terms + d1r[h, 0].astype(F32) + d1r[h, 1].astype(F32) + d1r[h, 2].astype(F32)
         cols = pl.ds(pl.multiple_of(h * D, D), D)
         drk_ref[:, cols] = terms[0].astype(BF16)
@@ -256,7 +258,7 @@
             score = dot(kr[tile], qs, NT) + jnp.concatenate([bias[tile]] * GROUP, 1)
             top = jnp.maximum(top, jnp.max(score, 0, keepdims=True))
             scores.append(score)
-        pl.when(h > 0)(lambda: step1(h - 1))
+        pl.when(h > 0)(lambda: step1(h - 1, 0))
         pl.when(h == 0)(lambda: relay_resp(h, 1))
         pl.when(h < HEADS - 2)(lambda: start_b(h + 2))
         top = top * SCALE_LOG2E
@@ -274,6 +276,14 @@
         VT[:, KEYS:] = vr.T
         probs = [weight * inv for weight in weights]
         halves = [prob.astype(BF16) for prob in probs]
+        for i in range(len(tiles)):
+            for_values = dot(halves[i], gs, NN).reshape(8, SIDE, 8, D)
+            AP[h, i // 2, 1, i % 2 * 8 : i % 2 * 8 + 8] = for_values
+        c0(h, 1).start()
+        for i in range(len(tiles)):
+            for_values = dot(halves[len(tiles) + i], gs, NN)
+            T[h, i, :, 1] = for_values.astype(BF16).reshape(2, RT, D)
+        d0(h, 1).start()
         out = functools.reduce(
             jnp.add, [dot(VT[:, i * TILE : (i + 1) * TILE], half, NN) for i, half in enumerate(halves)]
         )
@@ -286,25 +296,21 @@
         def tile_grads(i, values):
             ds = (probs[i] * (dot(values, gs, NT) - row_dot)).astype(BF16)
             DS[h % SLOTS, i * TILE : (i + 1) * TILE] = ds
-            return dot(ds, qs, NN), dot(halves[i], gs, NN)
+            return dot(ds, qs, NN)
 
         for i, tile in enumerate(tiles):
-            grads = tile_grads(i, vp[tile])
-            for t in (0, 1):
-                AP[h, i // 2, t, i % 2 * 8 : i % 2 * 8 + 8] = grads[t].reshape(8, SIDE, 8, D)
-        c0(h).start()
+            AP[h, i // 2, 0, i % 2 * 8 : i % 2 * 8 + 8] = tile_grads(i, vp[tile]).reshape(8, SIDE, 8, D)
+        c0(h, 0).start()
+        step1(h, 1)
         pl.when(h > 0)(lambda: step2(h - 1))
         for i, tile in enumerate(tiles):
-            for_keys, for_values = tile_grads(len(tiles) + i, vr[tile])
-            T[h, i, :, 0] = (for_keys * SCALE).astype(BF16).reshape(2, RT, D)
-            T[h, i, :, 1] = for_values.astype(BF16).reshape(2, RT, D)
-        d0(h).start()
+            T[h, i, :, 0] = (tile_grads(len(tiles) + i, vr[tile]) * SCALE).astype(BF16).reshape(2, RT, D)
+        d0(h, 0).start()
         return 0
 
     lax.fori_loop(0, HEADS, head, 0)
     dq_part(0)
-    step1_prompt(3)
-    step1_resp(3)
+    step1(3, 0)
     dq_part(1)
     step3(2)
     dq_part(2)
@@ -319,9 +325,10 @@
     def sent(h, _):
         a2_all(h).wait_send()
         a3(h).wait_send()
-        c1_all(h).wait_send()
-        c0(h).wait_send()
-        d0(h).wait_send()
+        for t in (0, 1):
+            c0(h, t).wait_send()
+            c1_all(h, t).wait_send()
+            d0(h, t).wait_send()
         b_sib(h, 0, 0).wait_send()
         b_sib(h, 1, 0).wait_send()
         for k in (1, 2, 3):
@@ -330,7 +337,8 @@
             def conditional(k=k):
                 b_sib(h, 0, k).wait_send()
                 b_sib(h, 1, k).wait_send()
-                d1(h, k).wait_send()
+                d1(h, 0, k).wait_send()
+                d1(h, 1, k).wait_send()
 
             pl.when(zh - k >= 0)(conditional)
 
@@ -372,15 +380,16 @@
         pltpu.VMEM((HEADS, 2, 2, PLANE, SIDE, 8, D), F32),
         pltpu.VMEM((HEADS, SIDE, 2, 2, RT, D), BF16),
         pltpu.VMEM((HEADS, 2, PLANE, SIDE, 8, D), F32),
-        pltpu.VMEM((HEADS, PLANE - 1, 2, SIDE, 8, D), F32),
+        pltpu.VMEM((HEADS, 2, PLANE - 1, SIDE, 8, D), F32),
         pltpu.VMEM((HEADS, 3, 2, 8, D), F32),
-        pltpu.VMEM((HEADS, SIDE, 2, RT, D), BF16),
+        pltpu.VMEM((HEADS, 2, SIDE, RT, D), BF16),
         pltpu.VMEM((HEADS, 3, 2, RT, D), BF16),
     ]
     per_peer = dma((HEADS, 3))
     per_head = dma((HEADS,))
     sems = [dma((2, 3))] * 2 + [per_head] * 4 + [dma((HEADS, 2, 3))] * 2 + [dma((HEADS, 2, 4))] * 2
-    sems += [per_head] * 4 + [per_peer] * 2 + [per_head] * 2 + [per_peer] * 2
+    per_type = dma((HEADS, 2))
+    sems += [per_type] * 4 + [per_peer] * 2 + [per_type] * 2 + [dma((HEADS, 2, 3))] * 2
     wide = jax.ShapeDtypeStruct(queries.shape[1:], BF16)
     rows = jax.ShapeDtypeStruct(response_key_rows.shape[1:], BF16)
     shared = jax.ShapeDtypeStruct(prompt_keys.shape, F32)

time: 88.4 us -> 83.1 us (0.940)
  Pallas kernels: 87.5 us -> 82 us
    pallas_call x1, Pallas kernels: 84.5 us -> 78.9 us  [body(): pl.pallas_call(kernel, out_shape=shapes, in_specs=[hbm] * 2 + [vmem] * 4...]
where the time goes in v2:
time: 83.1 us; the launch traced here: 82.8 us
  Pallas kernels  82 us (99%)
    pallas_call x1, Pallas kernels, body(): pl.pallas_call(kernel, out_shape=shapes, in_specs=[hbm] * 2 + [vmem] * 4...  78.9 us
    pallas_call x1, Pallas kernels, body(): pl.pallas_call(hand_over, out_shape=shapes, in_specs=[vmem] * 6, out_spec...  3.03 us

profile of v2, /device:TPU:8, one launch (start us, length us, event | category | flops | bytes accessed | tf_op | source)
XLA Modules:
  0.0 82.8 jit_solution(16706733535651756537)
XLA Ops:
  0.6 78.9 %shard_map.118 = (bf16[128,4096]{1,0:T(8,128)(2,1)}, bf16[128,4096]{1,0:T(8,128)(2,1)}, bf16[128,512]{1,0:T(8,128)(2,1)}, bf16[128,512]{1,0:T(8,128)(2,1)}, f32[8,512]{1,0:T(8,128)}, /*index=5*/f32[8,512]{1,0:T(8,128)}) custom-call(bf16[128,4096]{1,0:T(8,128)(2,1)} %bitcast.8, bf16[128,4096]{1,0:T(8,128)(2,1)} %bitcast.9, bf16[128,512]{1,0:T(8,128)(2,1)} %bitcast.12, ...), custom_call_target="tpu_custom_call" | custom-call | flops 12999999488 | bytes 5242880 | tf_op jit(solution)/shard_map/pallas_call | solution.py:397
  79.6 3.0 %shard_map.119 = (bf16[128,4096]{1,0:T(8,128)(2,1)}, bf16[128,4096]{1,0:T(8,128)(2,1)}, bf16[128,512]{1,0:T(8,128)(2,1)}, bf16[128,512]{1,0:T(8,128)(2,1)}, f32[8,512]{1,0:T(8,128)}, /*index=5*/f32[8,512]{1,0:T(8,128)}) custom-call(bf16[128,4096]{1,0:T(8,128)(2,1)} %get-tuple-element.18.refs_0_, bf16[128,4096]{1,0:T(8,128)(2,1)} %get-tuple-element.19.refs_1_, ...), custom_call_target="tpu_custom_call" | custom-call | tf_op jit(solution)/shard_map/pallas_call | solution.py:408

commit v3 on v2

--- a/solution.py
+++ b/solution.py
@@ -146,9 +146,15 @@
             pl.when(zh - k >= 0)(lambda k=k: b_sib(h, t, k).wait_recv())
 
     def step1(h, t):
+        step1_prompt(h, t)
+        step1_resp(h, t)
+
+    def step1_prompt(h, t):
         c0(h, t).wait_recv()
         AP[h, c, t] += c0r[h, t]
         c1_start(h, t)
+
+    def step1_resp(h, t):
         d0(h, t).wait_recv()
         for k in (1, 2, 3):
 
@@ -291,6 +297,7 @@
         for j, col in enumerate(cols):
             o_ref[:, col] = out[:, j * RT : (j + 1) * RT].T.astype(BF16)
         row_dot = jnp.sum(gs.astype(F32).T * out, 0, keepdims=True)
+        step1(h, 1)
         pl.when(h > 1)(lambda: step3(h - 2))
 
         def tile_grads(i, values):
@@ -301,7 +308,6 @@
         for i, tile in enumerate(tiles):
             AP[h, i // 2, 0, i % 2 * 8 : i % 2 * 8 + 8] = tile_grads(i, vp[tile]).reshape(8, SIDE, 8, D)
         c0(h, 0).start()
-        step1(h, 1)
         pl.when(h > 0)(lambda: step2(h - 1))
         for i, tile in enumerate(tiles):
             T[h, i, :, 0] = (tile_grads(len(tiles) + i, vr[tile]) * SCALE).astype(BF16).reshape(2, RT, D)
@@ -309,8 +315,9 @@
         return 0
 
     lax.fori_loop(0, HEADS, head, 0)
+    step1_prompt(3, 0)
     dq_part(0)
-    step1(3, 0)
+    step1_resp(3, 0)
     dq_part(1)
     step3(2)
     dq_part(2)
@@ -353,11 +360,26 @@
 
 
 def hand_over(*refs):
-    n = (len(refs) - 1) // 2
-    copies = [pltpu.make_async_copy(refs[i], refs[n + i], refs[-1].at[i]) for i in range(n)]
-    for copy in copies:
+    (sources, targets, buffers), (in_sems, out_sems) = (refs[i : i + 6] for i in (0, 6, 12)), refs[18:]
+    pieces = []
+    for i, source in enumerate(sources):
+        rows = source.shape[0]
+        step = 32 if source.shape[1] > HEADS * D else rows
+        pieces += [(i, slice(first, first + step)) for first in range(0, rows, step)]
+    arrive = [
+        pltpu.make_async_copy(sources[i].at[rows], buffers[i].at[rows], in_sems.at[n])
+        for n, (i, rows) in enumerate(pieces)
+    ]
+    leave = [
+        pltpu.make_async_copy(buffers[i].at[rows], targets[i].at[rows], out_sems.at[n])
+        for n, (i, rows) in enumerate(pieces)
+    ]
+    for copy in arrive:
         copy.start()
-    for copy in copies:
+    for before, after in zip(arrive, leave):
+        before.wait()
+        after.start()
+    for copy in leave:
         copy.wait()
 
 
@@ -408,9 +430,9 @@
     out, dq, drk, drv, dpk, dpv = pl.pallas_call(
         hand_over,
         out_shape=shapes,
-        in_specs=[vmem] * 6,
+        in_specs=[hbm] * 6,
         out_specs=[hbm] * 6,
-        scratch_shapes=[dma((6,))],
+        scratch_shapes=[pltpu.VMEM(shape.shape, shape.dtype) for shape in shapes] + [dma((12,)), dma((12,))],
     )(*results)
     return out[None], dq[None], drk[None], drv[None], dpk, dpv
 

time: 83.1 us -> 83 us (level)
  no operation moved by 1% of the time
where the time goes in v3:
time: 83 us; the launch traced here: 82.5 us
  Pallas kernels  81.7 us (98%)
    pallas_call x1, Pallas kernels, body(): pl.pallas_call(kernel, out_shape=shapes, in_specs=[hbm] * 2 + [vmem] * 4...  79.1 us
    pallas_call x1, Pallas kernels, body(): pl.pallas_call(hand_over, out_shape=shapes, in_specs=[hbm] * 6, out_specs...  2.55 us

profile of v3, /device:TPU:8, one launch (start us, length us, event | category | flops | bytes accessed | tf_op | source)
XLA Modules:
  0.0 82.5 jit_solution(15299445973151950088)
XLA Ops:
  0.6 79.1 %shard_map.118 = (bf16[128,4096]{1,0:T(8,128)(2,1)}, bf16[128,4096]{1,0:T(8,128)(2,1)}, bf16[128,512]{1,0:T(8,128)(2,1)}, bf16[128,512]{1,0:T(8,128)(2,1)}, f32[8,512]{1,0:T(8,128)}, /*index=5*/f32[8,512]{1,0:T(8,128)}) custom-call(bf16[128,4096]{1,0:T(8,128)(2,1)} %bitcast.8, bf16[128,4096]{1,0:T(8,128)(2,1)} %bitcast.9, bf16[128,512]{1,0:T(8,128)(2,1)} %bitcast.12, ...), custom_call_target="tpu_custom_call" | custom-call | flops 12999999488 | bytes 5242880 | tf_op jit(solution)/shard_map/pallas_call | solution.py:419
  79.8 2.6 %shard_map.119 = (bf16[128,4096]{1,0:T(8,128)(2,1)}, bf16[128,4096]{1,0:T(8,128)(2,1)}, bf16[128,512]{1,0:T(8,128)(2,1)}, bf16[128,512]{1,0:T(8,128)(2,1)}, f32[8,512]{1,0:T(8,128)}, /*index=5*/f32[8,512]{1,0:T(8,128)}) custom-call(bf16[128,4096]{1,0:T(8,128)(2,1)} %get-tuple-element.18.refs_0_, bf16[128,4096]{1,0:T(8,128)(2,1)} %get-tuple-element.19.refs_1_, ...), custom_call_target="tpu_custom_call" | custom-call | tf_op jit(solution)/shard_map/pallas_call | solution.py:430
